TPU v7x, 128 devices: a whole 4x4x4 slice. The times are simulated.
128 devices in a mesh: dp: 16 (over y, x), tensor: 8 (over z, core).
Axes of the slice: x: 4, y: 4, z: 4, core: 2. Of those that a mesh axis runs over, the one named last changes fastest.
Arguments:
- hidden_input: bfloat16 [16384, 8192], P('dp'), may hold values from -6 to 6
- key_value_gradient: bfloat16 [2, 16384, 1024], P(None, 'dp', 'tensor'), may hold values from -6 to 6
- key_value_weight: bfloat16 [2, 8192, 1024], P(None, None, 'tensor'), may hold values from -0.0625 to 0.0625
- down_adapters: bfloat16 [128, 32, 8192], P(None, None, 'tensor'), may hold values from -0.0625 to 0.0625
- up_adapters: bfloat16 [128, 2, 16, 1024], P(None, None, None, 'tensor'), may hold values from -0.1875 to 0.1875
- adapter_inner_saved: bfloat16 [32, 16384], P(None, 'dp'), may hold values from -2 to 2
- block_owner_tenant: int32 [128], P('dp'), may hold values from 0 to 127
- live_block_counts: int32 [16], P('dp'), may hold values from 1 to 8, as said below
- tenant_position: int32 [128], replicated, may hold values from 0 to 127, each once
Outputs:
- hidden_gradient: bfloat16 [16384, 8192], P('dp', 'tensor')
- grad_a: float32 [128, 32, 8192], P('dp', None, 'tensor')
- grad_b: float32 [128, 2, 16, 1024], P('dp', None, None, 'tensor')
Inputs may be any that keep to these rules, and one draw needn't show every extreme that they name: `live_block_counts`: some index of dp has all 8 block slots live.
All inputs are finite; a program needn't handle non-finite values.
Results may differ from a plain program's by a relative error of at most 0.022.
Values may be sent and summed in bfloat16 or wider, within the bound.
A program may use at most 192 MiB of HBM per device.

v0:
```python
import jax
import jax.numpy as jnp
from jax import lax
from jax.sharding import PartitionSpec as P


def per_device(
    hidden_input,
    key_value_gradient,
    key_value_weight,
    down_adapters,
    up_adapters,
    adapter_inner_saved,
    block_owner_tenant,
    live_block_counts,
    tenant_position,
):
    tok_rows = hidden_input.shape[0]
    block_list = block_owner_tenant.shape[0]
    block_length = tok_rows // block_list
    head_cols = key_value_gradient.shape[2]
    width_cols = down_adapters.shape[2]
    tenants = tenant_position.shape[0]
    rank_row_slice = down_adapters.shape[1]
    live_blk = jnp.arange(block_list, dtype=jnp.int32) < live_block_counts[0]
    live_tok = jnp.broadcast_to(live_blk[:, None], (block_list, block_length)).reshape(tok_rows)
    grad = key_value_gradient * live_tok.astype(jnp.bfloat16)[None, :, None]
    picked = block_owner_tenant[:, None] == jnp.arange(tenants, dtype=jnp.int32)[None, :]
    slot_blk = jnp.sum(jnp.where(picked, tenant_position[None, :], 0), axis=1)
    b_sel = jnp.take(up_adapters, block_owner_tenant, axis=0)
    g_blk = grad.reshape(2, block_list, block_length, head_cols)
    inner_part = jnp.einsum("cbij,bcrj->bicr", g_blk, b_sel, preferred_element_type=jnp.float32)
    inner = lax.psum(inner_part.reshape(tok_rows, rank_row_slice).astype(jnp.bfloat16), "tensor")
    inner_block = inner.reshape(block_list, block_length, rank_row_slice)
    selected_down = jnp.take(down_adapters, block_owner_tenant, axis=0)
    adapter_input_gradient = jnp.einsum(
        "hxr,hrg->hxg", inner_block, selected_down, preferred_element_type=jnp.float32
    ).reshape(tok_rows, width_cols)
    partial_value = jnp.einsum(
        "cnj,cdj->nd", grad, key_value_weight, preferred_element_type=jnp.float32
    )
    base_offset = lax.psum_scatter(
        partial_value.astype(jnp.bfloat16), "tensor", scatter_dimension=1, tiled=True
    ).astype(jnp.float32)
    hidden_gradient = (base_offset + 2.0 * adapter_input_gradient).astype(jnp.bfloat16)
    x_cols = lax.dynamic_slice_in_dim(
        hidden_input, lax.axis_index("tensor") * width_cols, width_cols, 1
    )
    per_a = jnp.einsum(
        "bic,bid->bcd",
        inner_block,
        x_cols.reshape(block_list, block_length, width_cols),
        preferred_element_type=jnp.float32,
    )
    hidden_block = adapter_inner_saved.reshape(2, rank_row_slice // 2, block_list, block_length)
    per_b = jnp.einsum("crbi,cbij->bcrj", hidden_block, g_blk, preferred_element_type=jnp.float32)
    per_block = 2.0 * jnp.concatenate(
        [per_a, per_b.reshape(block_list, rank_row_slice, head_cols)], axis=2
    )
    owned_rows = tenants // lax.axis_size("dp")
    onehot = (
        slot_blk[None, :] == jnp.arange(owned_rows * lax.axis_size("dp"), dtype=jnp.int32)[:, None]
    ).astype(jnp.float32)
    owned = lax.psum_scatter(
        jnp.einsum("sb,bcd->scd", onehot, per_block, precision=lax.Precision.HIGHEST).astype(
            jnp.bfloat16
        ),
        "dp",
        scatter_dimension=0,
        tiled=True,
    ).astype(jnp.float32)
    grad_a = owned[:, :, :width_cols]
    grad_b = owned[:, :, width_cols:].reshape(owned_rows, 2, rank_row_slice // 2, head_cols)
    return (hidden_gradient, grad_a, grad_b)


def solution(mesh):
    return jax.shard_map(
        per_device,
        mesh=mesh,
        in_specs=(
            P("dp", None),
            P(None, "dp", "tensor"),
            P(None, None, "tensor"),
            P(None, None, "tensor"),
            P(None, None, None, "tensor"),
            P(None, "dp"),
            P("dp"),
            P("dp"),
            P(),
        ),
        out_specs=(P("dp", "tensor"), P("dp", None, "tensor"), P("dp", None, None, "tensor")),
        check_vma=False,
    )
```

profile of v0, /device:TPU:1, one launch (start us, length us, event | category | flops | bytes accessed | tf_op | source)
XLA Modules:
  0.0 339.3 jit_solution(14579576244899069147)
XLA Ops:
  7.2 0.0 copy-start
  7.2 0.0 copy-start.5
  7.2 0.0 copy-start.6
  7.2 0.0 all-reduce.4.cloned.1.call-start
  7.2 0.7 compare_select_fusion
  8.0 0.7 compare_and_fusion
  9.3 0.1 broadcast_bitcast_fusion
  9.4 1.2 broadcast_multiply_fusion
  10.6 0.0 copy-done
  10.6 0.0 copy-start.2
  10.7 0.6 gather_fusion
  11.2 1.1 convolution_convert_fusion.1
  12.3 0.0 all-reduce.4.cloned.1.call-update
  12.3 0.0 all-reduce.6.cloned.1.call-start
  12.4 0.9 copy.32
  13.2 0.2 fusion.4
  13.5 0.0 copy-done.2
  13.5 1.8 constant_dynamic-slice_fusion
  15.2 0.0 copy-done.5
  15.2 0.0 copy-done.6
  15.3 0.2 select_reduce_fusion
  15.4 57.1 %all-reduce.4.cloned.1.call-done = bf16[8,128,32]{1,2,0:T(8,128)(2,1)} async-done(((bf16[8,128,32]{1,2,0:T(8,128)(2,1)}), bf16[8,128,32]{1,2,0:T(8,128)(2,1)}) %all-reduce.4.cloned.1.call-update) | async-done | bytes 65552 | tf_op jit(solution)/shard_map/psum | solution.py:33
  72.5 1.2 fusion.17
  73.8 0.1 maximum_multiply_fusion
  73.9 9.9 %convolution_convert_fusion = bf16[128,32,1152]{2,0,1:T(8,128)(2,1)} fusion(f32[8,32,1152]{2,1,0:T(8,128)S(1)} %maximum_multiply_fusion, s32[8]{0:T(128)S(1)} %select_reduce_fusion), kind=kOutput, calls=%fused_computation.3 | convolution fusion | flops 457704448 | bytes 10616864 | tf_op jit(solution)/shard_map/sb,bcd->scd/dot_general | solution.py:65
  83.8 0.0 copy-start.3
  83.8 0.0 all-reduce.6.cloned.1.call-update
  83.8 0.0 reduce-scatter.3.cloned.1.call-start
  83.8 1.0 copy-done.3
  84.8 10.8 %bitcast_convert_fusion = bf16[1024,8192]{1,0:T(8,128)(2,1)} fusion(bf16[2,1024,128]{2,1,0:T(8,128)(2,1)S(1)} %copy-done.3, bf16[2,8192,128]{2,1,0:T(8,128)(2,1)} %param.11), kind=kOutput, calls=%fused_computation.2 | convolution fusion | flops 4303355904 | bytes 21495808 | tf_op jit(solution)/shard_map/cnj,cdj->nd/dot_general | solution.py:39
  95.6 0.0 copy-start.7
  95.6 0.0 copy-start.4
  95.6 0.0 reduce-scatter.3.cloned.1.call-update
  95.6 4.0 %gather_fusion.1 = bf16[8,32,1024]{2,1,0:T(8,128)(2,1)S(1)} fusion(bf16[128,32,1024]{2,1,0:T(8,128)(2,1)} %param.12, s32[1024]{0:T(1024)S(1)} %pad_clamp_fusion), kind=kCustom, calls=%fused_computation.1 | custom fusion | bytes 1048608 | tf_op jit(solution)/shard_map/jit(_take)/gather | solution.py:35
  99.6 0.0 copy-done.7
  99.6 0.6 dynamic-slice
  100.9 0.0 copy-done.4
  100.9 2.7 convolution_multiply_fusion
  103.6 130.9 %all-reduce.6.cloned.1.call-done = bf16[128,32,1152]{2,0,1:T(8,128)(2,1)} async-done(((bf16[128,32,1152]{2,0,1:T(8,128)(2,1)}), bf16[128,32,1152]{2,0,1:T(8,128)(2,1)}) %all-reduce.6.cloned.1.call-update) | async-done | bytes 9437200
  234.5 1.1 dynamic-slice_convert_fusion
  235.6 0.1 slice.12
  235.8 1.6 copy.28
  237.3 0.0 copy-start.1
  237.3 0.7 copy.29
  238.0 89.8 %reduce-scatter.3.cloned.1.call-done = bf16[1024,1024]{1,0:T(8,128)(2,1)} async-done(((bf16[1024,8192]{1,0:T(8,128)(2,1)}), bf16[1024,1024]{1,0:T(8,128)(2,1)}) %reduce-scatter.3.cloned.1.call-update) | async-done | bytes 2097168 | tf_op jit(solution)/shard_map/reduce_scatter | solution.py:42
  327.8 5.0 %fusion = bf16[1024,1024]{1,0:T(8,128)(2,1)} fusion(f32[8,128,1024]{2,1,0:T(8,128)} %convolution_multiply_fusion, bf16[1024,1024]{1,0:T(8,128)(2,1)} %reduce-scatter.3.cloned.1.call-done), kind=kLoop, calls=%fused_computation.5 | loop fusion | flops 3145728 | bytes 8388608 | tf_op jit(solution)/shard_map/convert_element_type | solution.py:45
  332.8 0.0 copy-done.1
  (3 shorter events, 0.0 us)
Async XLA Ops:
  7.2 3.5 %copy-start = (bf16[128,2,16,128]{3,2,1,0:T(8,128)(2,1)S(1)}, bf16[128,2,16,128]{3,2,1,0:T(8,128)(2,1)}, u32[]{:S(2)}) copy-start(bf16[128,2,16,128]{3,2,1,0:T(8,128)(2,1)} %param.13) | copy-start | bytes 3145732
  7.2 8.1 %copy-start.5 = (s32[8]{0:T(128)S(1)}, s32[8]{0:T(128)}, u32[]{:S(2)}) copy-start(s32[8]{0:T(128)} %param.15) | copy-start | bytes 100
  7.2 8.1 %copy-start.6 = (s32[128]{0:T(128)S(1)}, s32[128]{0:T(128)}, u32[]{:S(2)}) copy-start(s32[128]{0:T(128)} %param.17) | copy-start | bytes 1540
  7.2 65.3 %all-reduce.4.cloned.1.call-start = ((), (), s32[]{:S(2)}) async-start(), calls=%async_computation.2 | async-start | bytes 131072 | tf_op jit(solution)/shard_map/psum | solution.py:33
  10.6 2.8 copy-start.2
  12.3 222.2 %all-reduce.6.cloned.1.call-start = ((), (), s32[]{:S(2)}) async-start(), calls=%async_computation.3 | async-start | bytes 18874368
  83.8 1.0 copy-start.3
  83.8 244.0 %reduce-scatter.3.cloned.1.call-start = ((), (), s32[]{:S(2)}) async-start(), calls=%async_computation.1 | async-start | bytes 18874368 | tf_op jit(solution)/shard_map/reduce_scatter | solution.py:42
  95.6 4.0 %copy-start.7 = (u32[128]{0:T(128)S(1)}, u32[128]{0:T(128)}, u32[]{:S(2)}) copy-start(u32[128]{0:T(128)} %constant.44) | copy-start | bytes 1540
  95.6 5.3 %copy-start.4 = (bf16[8,128,32]{1,2,0:T(8,128)(2,1)S(1)}, bf16[8,128,32]{1,2,0:T(8,128)(2,1)}, u32[]{:S(2)}) copy-start(bf16[8,128,32]{1,2,0:T(8,128)(2,1)} %all-reduce.4.cloned.1.call-done) | copy-start | bytes 196612
  237.3 95.4 %copy-start.1 = (bf16[128,2,16,128]{3,2,1,0:T(8,128)(2,1)S(1)}, bf16[128,2,16,128]{3,2,1,0:T(8,128)(2,1)}, u32[]{:S(2)}) copy-start(bf16[128,2,16,128]{3,2,1,0:T(8,128)(2,1)} %param.13) | copy-start | bytes 3145732
Sparse Core Ops, SparseCore 0:
  12.4 60.0 all-reduce.3
  83.9 150.5 all-reduce.5
  236.9 90.8 reduce-scatter.2
where the time goes:
time: 340 us; the launch traced here: 339 us
  waiting for transfers between devices  278 us (82%)
  matrix products  25.9 us (8%)
  between operations  15.2 us (4%)
  local copies, waits for them, and re-layouts  11.2 us (3%)
  other arithmetic  9.03 us (3%)
    unnamed x4, waiting for transfers between devices  131 us
    reduce_scatter x1, waiting for transfers between devices, per_device(): lax.psum_scatter(partial_value.astype(jnp.bfloat16), 'tensor', scatter_di...  89.8 us
    psum x1, waiting for transfers between devices, per_device(): lax.psum(inner_part.reshape(tok_rows, rank_row_slice).astype(jnp.bfloat16...  57.1 us
    dot_general x1, matrix products, per_device(): jnp.einsum('cnj,cdj->nd', grad, key_value_weight, preferred_element_type=...  10.8 us
    dot_general x1, matrix products, per_device(): jnp.einsum('sb,bcd->scd', onehot, per_block, precision=lax.Precision.HIGH...  9.89 us
  transfers between devices with their start and end apart: 3, of which 3 were waited for; matrix products, arithmetic and copies ran while one was open for 7% of the time, Pallas kernels for 0%

commit v1 on v0

--- a/solution.py
+++ b/solution.py
@@ -30,7 +30,9 @@
     b_sel = jnp.take(up_adapters, block_owner_tenant, axis=0)
     g_blk = grad.reshape(2, block_list, block_length, head_cols)
     inner_part = jnp.einsum("cbij,bcrj->bicr", g_blk, b_sel, preferred_element_type=jnp.float32)
-    inner = lax.psum(inner_part.reshape(tok_rows, rank_row_slice).astype(jnp.bfloat16), "tensor")
+    inner = jax.lax.all_gather(
+        inner_part.reshape(tok_rows, rank_row_slice).astype(jnp.bfloat16), axis_name="tensor"
+    ).sum(axis=0)
     inner_block = inner.reshape(block_list, block_length, rank_row_slice)
     selected_down = jnp.take(down_adapters, block_owner_tenant, axis=0)
     adapter_input_gradient = jnp.einsum(

time: 340 us -> 209 us (0.61)
  waiting for transfers between devices: 278 us -> 132 us
  blocking collectives: 0 us -> 15.7 us
    reduce_scatter x1, waiting for transfers between devices: 89.8 us -> 0.01 us  [per_device(): lax.psum_scatter(partial_value.astype(jnp.bfloat16), 'tensor', scatter_di...]
    psum x1 -> x0, waiting for transfers between devices: 57.1 us -> none  [per_device(): lax.psum(inner_part.reshape(tok_rows, rank_row_slice).astype(jnp.bfloat16...]
    all_gather x0 -> x1, blocking collectives: none -> 15.7 us  [per_device(): jax.lax.all_gather(inner_part.reshape(tok_rows, rank_row_slice).astype(jn...]
    unnamed x4 -> x3, waiting for transfers between devices: 131 us -> 132 us
  transfers between devices with their start and end apart: 3 -> 2, of which waited for: 3 -> 1; matrix products, arithmetic and copies ran while one was open for 7% -> 10% of each run, Pallas kernels for 0% -> 0%
where the time goes in v1:
time: 209 us
  waiting for transfers between devices  132 us (63%)
  matrix products  24.5 us (12%)
  between operations  16.9 us (8%)
  blocking collectives  15.7 us (8%)
  local copies, waits for them, and re-layouts  10.3 us (5%)
  other arithmetic  9.79 us (5%)
    unnamed x3, waiting for transfers between devices  132 us
    all_gather x1, blocking collectives, per_device(): jax.lax.all_gather(inner_part.reshape(tok_rows, rank_row_slice).astype(jn...  15.7 us
    dot_general x1, matrix products, per_device(): jnp.einsum('cnj,cdj->nd', grad, key_value_weight, preferred_element_type=...  10.8 us
    dot_general x1, matrix products, per_device(): jnp.einsum('sb,bcd->scd', onehot, per_block, precision=lax.Precision.HIGH...  9.92 us
    convert_element_type x1, other arithmetic, per_device(): (base_offset + 2.0 * adapter_input_gradient).astype(jnp.bfloat16)  4.96 us
  transfers between devices with their start and end apart: 2, of which 1 were waited for; matrix products, arithmetic and copies ran while one was open for 10% of the time, Pallas kernels for 0%

profile of v1, /device:TPU:1, one launch (start us, length us, event | category | flops | bytes accessed | tf_op | source)
XLA Modules:
  0.0 208.9 jit_solution(17683692758144842754)
XLA Ops:
  8.0 0.0 copy-start
  8.0 0.0 all-reduce.3.cloned.1.call-start
  8.1 0.7 compare_select_fusion
  8.8 0.7 compare_and_fusion
  10.1 0.1 broadcast_bitcast_fusion
  10.2 1.2 broadcast_multiply_fusion
  11.4 0.0 copy-done
  11.5 0.6 gather_fusion
  12.0 0.4 fusion.2
  12.4 0.1 copy.36
  12.5 15.7 %all_gather.4 = bf16[8,1024,32]{1,2,0:T(8,128)(2,1)S(1)} all-gather(bf16[1,1024,32]{1,2,0:T(8,128)(2,1)S(1)} %convert_element_type.51), channel_id=1, replica_groups=mesh['dp'=16,'tensor'=8] {'tensor'}, dimensions={0}, use_global_device_ids=true | all-gather | bytes 589824 | tf_op jit(solution)/shard_map/all_gather | solution.py:33
  28.2 0.8 copy.47
  29.0 0.2 fusion.5
  29.3 0.9 select_reduce_fusion
  30.1 0.1 reduce_sum.21
  30.2 1.8 constant_dynamic-slice_fusion
  32.0 0.4 fusion.9
  32.4 0.1 maximum_multiply_fusion
  32.5 9.9 %convolution_convert_fusion = bf16[128,32,1152]{2,0,1:T(8,128)(2,1)} fusion(f32[8,32,1152]{2,1,0:T(8,128)S(1)} %maximum_multiply_fusion, s32[8]{0:T(128)S(1)} %select_reduce_fusion), kind=kOutput, calls=%fused_computation.3 | convolution fusion | flops 457704448 | bytes 10616864 | tf_op jit(solution)/shard_map/sb,bcd->scd/dot_general | solution.py:67
  42.4 0.0 all-reduce.3.cloned.1.call-update
  42.5 0.0 reduce-scatter.3.cloned.1.call-start
  42.5 10.8 %bitcast_convert_fusion = bf16[1024,8192]{1,0:T(8,128)(2,1)} fusion(bf16[2,1024,128]{2,1,0:T(8,128)(2,1)S(1)} %broadcast_multiply_fusion, bf16[2,8192,128]{2,1,0:T(8,128)(2,1)} %param.11), kind=kOutput, calls=%fused_computation.2 | convolution fusion | flops 4303355904 | bytes 21495808 | tf_op jit(solution)/shard_map/cnj,cdj->nd/dot_general | solution.py:41
  53.3 0.0 copy-start.2
  53.3 0.0 reduce-scatter.3.cloned.1.call-update
  53.3 4.0 %gather_fusion.1 = bf16[8,32,1024]{2,1,0:T(8,128)(2,1)S(1)} fusion(bf16[128,32,1024]{2,1,0:T(8,128)(2,1)} %param.12, s32[1024]{0:T(1024)S(1)} %pad_clamp_fusion), kind=kCustom, calls=%fused_computation.1 | custom fusion | bytes 1048608 | tf_op jit(solution)/shard_map/jit(_take)/gather | solution.py:37
  57.3 0.0 copy-done.2
  57.3 0.6 dynamic-slice
  58.5 2.7 %convolution_multiply_fusion = f32[8,128,1024]{2,1,0:T(8,128)} fusion(bf16[8,32,1024]{2,1,0:T(8,128)(2,1)S(1)} %gather_fusion.1, pred[8]{0:T(512)(128)(4,1)S(1)} %compare_and_fusion, bf16[1024,32]{0,1:T(8,128)(2,1)S(1)} %reduce_sum.21), kind=kOutput, calls=%fused_computation.6 | convolution fusion | flops 68419584 | bytes 4784136 | tf_op jit(solution)/shard_map/hxr,hrg->hxg/dot_general | solution.py:38
  61.3 131.6 %all-reduce.3.cloned.1.call-done = bf16[128,32,1152]{2,0,1:T(8,128)(2,1)} async-done(((bf16[128,32,1152]{2,0,1:T(8,128)(2,1)}), bf16[128,32,1152]{2,0,1:T(8,128)(2,1)}) %all-reduce.3.cloned.1.call-update) | async-done | bytes 9437200
  192.9 1.1 dynamic-slice_convert_fusion
  194.0 0.1 slice.12
  194.2 1.6 copy.42
  195.8 0.0 copy-start.1
  195.8 0.7 copy.43
  196.4 0.0 reduce-scatter.3.cloned.1.call-done
  196.4 5.0 %fusion = bf16[1024,1024]{1,0:T(8,128)(2,1)} fusion(f32[8,128,1024]{2,1,0:T(8,128)} %convolution_multiply_fusion, bf16[1024,1024]{1,0:T(8,128)(2,1)} %reduce-scatter.3.cloned.1.call-done), kind=kLoop, calls=%fused_computation.5 | loop fusion | flops 3145728 | bytes 8388608 | tf_op jit(solution)/shard_map/convert_element_type | solution.py:47
  201.4 0.0 copy-done.1
  (4 shorter events, 0.1 us)
Async XLA Ops:
  8.0 3.5 %copy-start = (bf16[128,2,16,128]{3,2,1,0:T(8,128)(2,1)S(1)}, bf16[128,2,16,128]{3,2,1,0:T(8,128)(2,1)}, u32[]{:S(2)}) copy-start(bf16[128,2,16,128]{3,2,1,0:T(8,128)(2,1)} %param.13) | copy-start | bytes 3145732
  8.0 184.9 %all-reduce.3.cloned.1.call-start = ((), (), s32[]{:S(2)}) async-start(), calls=%async_computation.2 | async-start | bytes 18874368
  42.5 154.0 %reduce-scatter.3.cloned.1.call-start = ((), (), s32[]{:S(2)}) async-start(), calls=%async_computation.1 | async-start | bytes 18874368 | tf_op jit(solution)/shard_map/reduce_scatter | solution.py:44
  53.3 4.0 %copy-start.2 = (u32[128]{0:T(128)S(1)}, u32[128]{0:T(128)}, u32[]{:S(2)}) copy-start(u32[128]{0:T(128)} %constant.47) | copy-start | bytes 1540
  195.8 5.6 %copy-start.1 = (bf16[128,2,16,128]{3,2,1,0:T(8,128)(2,1)S(1)}, bf16[128,2,16,128]{3,2,1,0:T(8,128)(2,1)}, u32[]{:S(2)}) copy-start(bf16[128,2,16,128]{3,2,1,0:T(8,128)(2,1)} %param.13) | copy-start | bytes 3145732
Sparse Core Ops, SparseCore 0:
  42.6 150.2 all-reduce.2
Sparse Core Ops, SparseCore 1:
  53.4 91.9 reduce-scatter.2
